TPU v7x, 32 devices: a whole 2x2x4 slice. The times are simulated.
32 devices in a mesh: sec: 4 (over x, core), tile: 8 (over z, y).
Axes of the slice: x: 2, y: 2, z: 4, core: 2. Of those that a mesh axis runs over, the one named last changes fastest.
Arguments:
- intersection_faces: bfloat16 [256, 1, 128, 128], P(('sec', 'tile')), may hold values from -6 to 6
- destination: int32 [256, 1], P(('sec', 'tile')), may hold values from 0 to 7; in each aligned block of 8 rows (0 to 7, 8 to 15, ...) at most 2 rows name the same one
- partner: int32 [256], P(('sec', 'tile')), may hold values from 0 to 7
- face_peaks: int32 [256, 2, 8], P(('sec', 'tile')), may hold values from 0 to 127
- coarse: bfloat16 [64, 256, 256], P(('sec', 'tile')), may hold values from -6 to 6
- coarse_peaks: int32 [256, 2, 8], P(('sec', 'tile')), may hold values from 0 to 255
- upper_faces: bfloat16 [64, 1, 128, 128], P(('sec', 'tile')), may hold values from -6 to 6
- lower_faces: bfloat16 [64, 1, 128, 128], P(('sec', 'tile')), may hold values from -6 to 6
- section_peaks: int32 [64, 2, 8], P(('sec', 'tile')), may hold values from 0 to 127
Outputs:
- fine_scores: float32 [256, 1, 8], P(('sec', 'tile'))
- coarse_scores: float32 [256, 8], P(('sec', 'tile'))
- section_scores: float32 [64, 1, 8], P(('sec', 'tile'))
Inputs may be any that keep to these rules, and one draw needn't show every extreme that they name: `destination`: in each aligned block of 8 rows (the faces of one device) no value appears more than 2 times.
All inputs are finite; a program needn't handle non-finite values.
Results may differ from a plain program's by a relative error of at most 0.012.
The roundings to bfloat16 on the way count: a program that leaves them out, or rounds other values in their place, can miss the bound.
Values may be sent and summed in bfloat16 or wider, within the bound.
A program may use at most 64 MiB of HBM per device.

v0:
```python
import jax
import jax.numpy as jnp
from jax import lax
from jax.sharding import PartitionSpec as P

TWO_PI = 6.283185307179586


def from_behind(value, axis, steps):
    count = lax.axis_size(axis)
    first, last = (max(0, -steps), min(count, count - steps))
    return lax.ppermute(value, axis, [(source, source + steps) for source in range(first, last)])


def window_weights(extent):
    positions = jnp.arange(extent, dtype=jnp.float32)
    return 0.5 - 0.5 * jnp.cos((positions + 0.5) * (TWO_PI / extent))


def dft_tables(extent):
    indices = jnp.arange(extent, dtype=jnp.int32)
    angles = (indices[:, None] * indices[None, :] % extent).astype(jnp.float32) * (TWO_PI / extent)
    return (jnp.cos(angles).astype(jnp.bfloat16), jnp.sin(angles).astype(jnp.bfloat16))


def spectrum(images):
    extent = images.shape[-1]
    weights = window_weights(extent)
    shaped = (images.astype(jnp.float32) * weights[:, None] * weights[None, :]).astype(jnp.bfloat16)
    cosine, sine_table = dft_tables(extent)
    segment_tables = jnp.stack([cosine, sine_table])
    segment_one = jnp.einsum(
        "jkx,...xy->...jky", segment_tables, shaped, preferred_element_type=jnp.float32
    ).astype(jnp.bfloat16)
    second_tables = jnp.stack(
        [
            jnp.concatenate([cosine, sine_table], axis=1),
            jnp.concatenate([-sine_table, cosine], axis=1),
        ]
    )
    segment_two = jnp.einsum(
        "...jky,jyl->...kl", segment_one, second_tables, preferred_element_type=jnp.float32
    )
    return (segment_two[..., :extent], -segment_two[..., extent:])


def correlate(own_spec, other_spec, peak_marks):
    own_real, own_imag = own_spec
    other_real, other_imag = other_spec
    cross_real = own_real * other_real + own_imag * other_imag
    cross_imag = own_imag * other_real - own_real * other_imag
    magnitude = jnp.sqrt(cross_real * cross_real + cross_imag * cross_imag)
    floor_value = 0.05 * jnp.mean(magnitude, axis=(-2, -1), keepdims=True) + 1e-06
    divisor = jnp.maximum(magnitude, floor_value)
    unit_real = cross_real / divisor
    unit_imag = cross_imag / divisor
    extent = own_real.shape[-1]
    indices = jnp.arange(extent, dtype=jnp.int32)
    row_angles = (peak_marks[..., 0, :, None] * indices % extent).astype(jnp.float32) * (
        TWO_PI / extent
    )
    col_angles = (peak_marks[..., 1, :, None] * indices % extent).astype(jnp.float32) * (
        TWO_PI / extent
    )
    row_cos = jnp.cos(row_angles)
    row_sin = jnp.sin(row_angles)
    high = lax.Precision.HIGHEST
    first_real = jnp.einsum("...pk,...kl->...pl", row_cos, unit_real, precision=high) - jnp.einsum(
        "...pk,...kl->...pl", row_sin, unit_imag, precision=high
    )
    first_imag = jnp.einsum("...pk,...kl->...pl", row_cos, unit_imag, precision=high) + jnp.einsum(
        "...pk,...kl->...pl", row_sin, unit_real, precision=high
    )
    return (
        jnp.sum(first_real * jnp.cos(col_angles) - first_imag * jnp.sin(col_angles), axis=-1)
        / extent
    )


def body(
    intersection_faces,
    destination,
    partner,
    face_peaks,
    coarse,
    coarse_peaks,
    upper_faces,
    lower_faces,
    section_peaks,
):
    face_dev = intersection_faces.shape[0]
    tile_dev = coarse.shape[0]
    per_tile = face_dev // tile_dev
    windows = intersection_faces.shape[1]
    peak_count = face_peaks.shape[2]
    coarse_side = coarse.shape[-1]
    tile_count = lax.axis_size("tile")
    capacity = max(2, (face_dev + tile_count - 1) // tile_count)
    slot_count = tile_count * capacity
    target = destination[:, 0]
    face_order = jnp.arange(face_dev, dtype=jnp.int32)
    earlier = (target[None, :] == target[:, None]) & (face_order[None, :] < face_order[:, None])
    position = jnp.sum(earlier.astype(jnp.int32), axis=1)
    slot_of = target * capacity + position
    slot_match = slot_of[None, :] == jnp.arange(slot_count, dtype=jnp.int32)[:, None]
    filled = jnp.any(slot_match, axis=1)
    source = jnp.sum(jnp.where(slot_match, face_order[None, :], 0), axis=1)
    requests = jnp.where(filled, partner[source] + 1, 0).reshape(tile_count, capacity)
    own_real, own_imag = spectrum(intersection_faces)
    parcel = jnp.where(
        filled[:, None, None, None],
        intersection_faces[source],
        jnp.zeros_like(intersection_faces[source]),
    )
    parcel = parcel.reshape((tile_count, capacity) + intersection_faces.shape[1:])
    peak_marks = face_peaks[source].reshape((tile_count, capacity) + face_peaks.shape[1:])
    got_faces, got_marks, wanted_ids = (
        lax.all_to_all(parcel, "tile", split_axis=0, concat_axis=0, tiled=True),
        lax.all_to_all(peak_marks, "tile", split_axis=0, concat_axis=0, tiled=True),
        lax.all_to_all(requests, "tile", split_axis=0, concat_axis=0, tiled=True),
    )

    def one_slot(packed):
        face_in, mark_in, wanted = packed
        chosen_slot = jnp.maximum(wanted - 1, 0)
        own_part = (own_real[chosen_slot], own_imag[chosen_slot])
        marks_all = mark_in[None]
        scores = correlate(spectrum(face_in), own_part, marks_all)
        return jnp.where(wanted > 0, scores, jnp.zeros_like(scores))

    slot_scores = lax.map(
        one_slot,
        (
            got_faces.reshape((slot_count,) + intersection_faces.shape[1:]),
            got_marks.reshape((slot_count,) + face_peaks.shape[1:]),
            wanted_ids.reshape(slot_count),
        ),
    )
    returned = lax.all_to_all(
        slot_scores.reshape(tile_count, capacity, windows, peak_count),
        "tile",
        split_axis=0,
        concat_axis=0,
        tiled=True,
    )
    fine_scores = returned.reshape(slot_count, windows, peak_count)[slot_of]
    coarse_real, coarse_imag = spectrum(coarse)
    wanted_tile = target * tile_dev + partner // per_tile
    empty_tiles = jnp.zeros((face_dev, coarse_side, coarse_side), jnp.bfloat16)
    shard_rows = lax.all_gather(coarse, "tile", axis=0, tiled=True)
    row_count = shard_rows.shape[0]
    inside = (wanted_tile >= 0) & (wanted_tile < row_count)
    selected = shard_rows[jnp.clip(wanted_tile, 0, row_count - 1)]
    partner_tiles = jnp.where(inside[:, None, None], selected, empty_tiles)

    def coarse_one(packed):
        tile_slot, other_tile, mark_in = packed
        return correlate(
            (coarse_real[tile_slot], coarse_imag[tile_slot]), spectrum(other_tile), mark_in
        )

    coarse_scores = lax.map(coarse_one, (face_order // per_tile, partner_tiles, coarse_peaks))
    lower_in = from_behind(lower_faces, "sec", 1)
    section_marks = section_peaks[:, None]
    section_scores = correlate(spectrum(upper_faces), spectrum(lower_in), section_marks)
    return (fine_scores, coarse_scores, section_scores)


def solution(mesh):
    return jax.shard_map(
        body,
        mesh=mesh,
        in_specs=(
            P(("sec", "tile"), None, None, None),
            P(("sec", "tile"), None),
            P(("sec", "tile")),
            P(("sec", "tile"), None, None),
            P(("sec", "tile"), None, None),
            P(("sec", "tile"), None, None),
            P(("sec", "tile"), None, None, None),
            P(("sec", "tile"), None, None, None),
            P(("sec", "tile"), None, None),
        ),
        out_specs=(
            P(("sec", "tile"), None, None),
            P(("sec", "tile"), None),
            P(("sec", "tile"), None, None),
        ),
        check_vma=False,
    )
```

profile of v0, /device:TPU:0, one launch (start us, length us, event | category | flops | bytes accessed | tf_op | source)
XLA Modules:
  0.0 286.7 jit_solution(2886775491009147244)
XLA Ops:
  7.9 0.9 convert_reduce_fusion
  9.7 1.3 gather_fusion
  11.7 7.3 %all-to-all-start = ((s32[8,1,2]{2,1,0:T(1,128)}), s32[8,1,2]{2,1,0:T(1,128)}, u32[]{:S(2)}, u32[]{:S(2)}) async-start(s32[8,1,2]{2,1,0:T(1,128)} %bitcast.34), calls=%async_computation | async-start | bytes 8192 | tf_op jit(solution)/shard_map/all_to_all | solution.py:120
  19.0 2.1 collective-permute-start
  22.5 1.2 compare_and_fusion
  24.5 1.0 fusion.221
  25.5 1.1 sine_convert_fusion.5
  26.6 1.1 sine_convert_fusion.4
  27.7 1.4 fusion.275
  33.8 0.9 fusion.155
  34.7 1.6 broadcast_select_fusion.2
  36.8 1.3 gather_fusion.1
  38.1 5.8 %all-to-all-start.1 = ((s32[8,2,2,8]{3,2,1,0:T(2,128)}), s32[8,2,2,8]{3,2,1,0:T(2,128)S(1)}, u32[]{:S(2)}, u32[]{:S(2)}) async-start(s32[8,2,2,8]{3,2,1,0:T(2,128)} %bitcast.35), calls=%async_computation.1 | async-start | bytes 32768 | tf_op jit(solution)/shard_map/all_to_all | solution.py:119
  44.5 1.3 reduce.15
  45.9 1.4 convolution_bitcast_fusion.4
  47.4 3.3 %all-to-all-done.1 = s32[8,2,2,8]{3,2,1,0:T(2,128)S(1)} async-done(((s32[8,2,2,8]{3,2,1,0:T(2,128)}), s32[8,2,2,8]{3,2,1,0:T(2,128)S(1)}, u32[]{:S(2)}, u32[]{:S(2)}) %all-to-all-start.1) | async-done | bytes 1056 | tf_op jit(solution)/shard_map/all_to_all | solution.py:119
  50.7 3.5 %all-to-all-start.2 = ((bf16[8,2,1,128,128]{3,4,1,2,0:T(8,128)(2,1)}), bf16[8,2,1,128,128]{3,4,1,2,0:T(8,128)(2,1)S(1)}, u32[]{:S(2)}, u32[]{:S(2)}) async-start(bf16[8,2,1,128,128]{3,4,1,2,0:T(8,128)(2,1)} %broadcast_select_fusion.2), calls=%async_computation.2 | async-start | bytes 1048576 | tf_op jit(solution)/shard_map/all_to_all | solution.py:118
  55.7 17.7 %all-to-all-done.2 = bf16[8,2,1,128,128]{3,4,1,2,0:T(8,128)(2,1)S(1)} async-done(((bf16[8,2,1,128,128]{3,4,1,2,0:T(8,128)(2,1)}), bf16[8,2,1,128,128]{3,4,1,2,0:T(8,128)(2,1)S(1)}, u32[]{:S(2)}, u32[]{:S(2)}) %all-to-all-start.2) | async-done | bytes 524320 | tf_op jit(solution)/shard_map/all_to_all | solution.py:118
  73.4 112.0 %while.24 = (s32[]{:T(128)}, f32[16,1,8]{2,1,0:T(1,128)}, s32[16]{0:T(128)S(1)}, s32[16,2,8]{2,1,0:T(2,128)S(1)}, bf16[16,1,128,128]{2,3,1,0:T(8,128)(2,1)S(1)},...) while((s32[]{:T(128)}, f32[16,1,8]{2,1,0:T(1,128)}, ...), condition=%wide.region_6.7_spmd, body=%wide.region_3.6_spmd.sunk | while | flops 33161740 | bytes 1723514 | solution.py:131
  76.9 1.5 fusion.332
  83.9 1.5 fusion.332
  90.9 1.5 fusion.332
  97.8 1.5 fusion.332
  104.8 1.5 fusion.332
  111.8 1.5 fusion.332
  118.8 1.5 fusion.332
  125.8 1.5 fusion.332
  132.8 1.5 fusion.332
  139.8 1.5 fusion.332
  146.7 1.5 fusion.332
  153.8 1.5 fusion.332
  160.8 1.5 fusion.332
  167.8 1.5 fusion.332
  174.8 1.5 fusion.332
  181.8 1.5 fusion.332
  185.4 3.6 %all-to-all-start.3 = ((f32[8,2,1,8]{3,1,2,0:T(2,128)}), f32[8,2,1,8]{3,1,2,0:T(2,128)S(1)}, u32[]{:S(2)}, u32[]{:S(2)}) async-start(f32[8,2,1,8]{3,1,2,0:T(2,128)} %bitcast.56), calls=%async_computation.3 | async-start | bytes 16384 | tf_op jit(solution)/shard_map/all_to_all | solution.py:139
  189.6 5.7 %all-to-all-done.3 = f32[8,2,1,8]{3,1,2,0:T(2,128)S(1)} async-done(((f32[8,2,1,8]{3,1,2,0:T(2,128)}), f32[8,2,1,8]{3,1,2,0:T(2,128)S(1)}, u32[]{:S(2)}, u32[]{:S(2)}) %all-to-all-start.3) | async-done | bytes 544 | tf_op jit(solution)/shard_map/all_to_all | solution.py:139
  195.3 1.3 gather_fusion.3
  196.6 2.3 gather_fusion.4
  199.1 80.1 %while.25 = (s32[]{:T(128)}, f32[8,8]{1,0:T(8,128)S(1)}, s32[8,2,8]{2,1,0:T(2,128)}, s32[8]{0:T(128)S(1)}, f32[2,256,256]{2,1,0:T(8,128)S(1)}, /*index=5*/bf16[8...) while((s32[]{:T(128)}, f32[8,8]{1,0:T(8,128)S(1)}, ...), condition=%wide.region_10.11_spmd, body=%wide.region_7.10_spmd.sunk | while | flops 232903680 | bytes 6737723 | solution.py:162
  202.4 1.0 fusion.348
  203.4 1.1 sine_convert_fusion.15
  204.5 1.1 sine_convert_fusion.14
  212.4 1.0 fusion.348
  213.4 1.1 sine_convert_fusion.15
  214.5 1.1 sine_convert_fusion.14
  222.4 1.0 fusion.348
  223.4 1.1 sine_convert_fusion.15
  224.5 1.1 sine_convert_fusion.14
  232.4 1.0 fusion.348
  233.4 1.1 sine_convert_fusion.15
  234.5 1.1 sine_convert_fusion.14
  242.5 1.0 fusion.348
  243.4 1.1 sine_convert_fusion.15
  244.6 1.1 sine_convert_fusion.14
  252.5 1.0 fusion.348
  253.5 1.1 sine_convert_fusion.15
  254.6 1.1 sine_convert_fusion.14
  262.5 1.0 fusion.348
  263.5 1.1 sine_convert_fusion.15
  264.6 1.1 sine_convert_fusion.14
  272.5 1.0 fusion.348
  273.5 1.1 sine_convert_fusion.15
  274.6 1.1 sine_convert_fusion.14
  (436 shorter events, 102.3 us)
Async XLA Ops:
  7.2 29.6 %copy-start = (s32[8,2,8]{2,1,0:T(2,128)S(1)}, s32[8,2,8]{2,1,0:T(2,128)}, u32[]{:S(2)}) copy-start(s32[8,2,8]{2,1,0:T(2,128)} %param.16) | copy-start | bytes 1540
  7.2 23.1 %copy-start.4 = (bf16[2,256,256]{2,1,0:T(8,128)(2,1)S(1)}, bf16[2,256,256]{2,1,0:T(8,128)(2,1)}, u32[]{:S(2)}) copy-start(bf16[2,256,256]{2,1,0:T(8,128)(2,1)} %param.17) | copy-start | bytes 786436
  7.2 189.4 %all-gather.2.cloned.1.call-start = ((), (), s32[]{:S(2)}) async-start(), calls=%async_computation.4 | async-start | bytes 2359296 | tf_op jit(solution)/shard_map/all_gather | solution.py:150
  9.7 23.2 %copy-start.7 = (s32[1024]{0:T(1024)}, s32[1024]{0:T(1024)S(1)}, u32[]{:S(2)}) copy-start(s32[1024]{0:T(1024)S(1)} %pad_clamp_fusion.2) | copy-start | bytes 12292
  11.7 26.4 %all-to-all-start = ((s32[8,1,2]{2,1,0:T(1,128)}), s32[8,1,2]{2,1,0:T(1,128)}, u32[]{:S(2)}, u32[]{:S(2)}) async-start(s32[8,1,2]{2,1,0:T(1,128)} %bitcast.34), calls=%async_computation | async-start | bytes 8192 | tf_op jit(solution)/shard_map/all_to_all | solution.py:120
  19.0 26.9 %collective-permute-start = (bf16[2,1,128,128]{3,2,1,0:T(8,128)(2,1)}, bf16[2,1,128,128]{3,2,1,0:T(8,128)(2,1)}, u32[]{:S(2)}, u32[]{:S(2)}) collective-permute-start(bf16[2,1,128,128]{3,2,1,0:T(8,128)(2,1)} %param.20), channel_id=1, source_target_pairs={{0,8},{8,16},{16,24},{1,9},{9,17},{17,25},{2,10},{10,18},{18,26},{... | collective-permute-start | bytes 196616 | tf_op jit(solution)/shard_map/ppermute | solution.py:12
  24.2 8.7 %copy-start.2 = (bf16[1,128,128]{2,1,0:T(8,128)(2,1)}, bf16[1,128,128]{2,1,0:T(8,128)(2,1)S(1)}, u32[]{:S(2)}) copy-start(bf16[1,128,128]{2,1,0:T(8,128)(2,1)S(1)} %get-tuple-element.303) | copy-start | bytes 98308
  24.2 8.7 %copy-start.3 = (bf16[1,128,128]{2,1,0:T(8,128)(2,1)}, bf16[1,128,128]{2,1,0:T(8,128)(2,1)S(1)}, u32[]{:S(2)}) copy-start(bf16[1,128,128]{2,1,0:T(8,128)(2,1)S(1)} %get-tuple-element.304) | copy-start | bytes 98308
  30.3 1.0 copy-start.5
  31.2 1.0 copy-start.1
  34.7 20.3 %copy-start.6 = (s32[2,1,1,8]{3,2,0,1:T(1,128)S(1)}, s32[2,1,1,8]{3,2,0,1:T(1,128)}, u32[]{:S(2)}) copy-start(s32[2,1,1,8]{3,2,0,1:T(1,128)} %get-tuple-element.299) | copy-start | bytes 196
  38.1 12.6 %all-to-all-start.1 = ((s32[8,2,2,8]{3,2,1,0:T(2,128)}), s32[8,2,2,8]{3,2,1,0:T(2,128)S(1)}, u32[]{:S(2)}, u32[]{:S(2)}) async-start(s32[8,2,2,8]{3,2,1,0:T(2,128)} %bitcast.35), calls=%async_computation.1 | async-start | bytes 32768 | tf_op jit(solution)/shard_map/all_to_all | solution.py:119
  50.7 22.7 %all-to-all-start.2 = ((bf16[8,2,1,128,128]{3,4,1,2,0:T(8,128)(2,1)}), bf16[8,2,1,128,128]{3,4,1,2,0:T(8,128)(2,1)S(1)}, u32[]{:S(2)}, u32[]{:S(2)}) async-start(bf16[8,2,1,128,128]{3,4,1,2,0:T(8,128)(2,1)} %broadcast_select_fusion.2), calls=%async_computation.2 | async-start | bytes 1048576 | tf_op jit(solution)/shard_map/all_to_all | solution.py:118
  185.4 13.5 %copy-start.8 = (pred[8]{0:T(512)(128)(4,1)S(1)}, pred[8]{0:T(512)(128)(4,1)}, u32[]{:S(2)}) copy-start(pred[8]{0:T(512)(128)(4,1)} %get-tuple-element.265) | copy-start | bytes 28
  185.4 9.9 %all-to-all-start.3 = ((f32[8,2,1,8]{3,1,2,0:T(2,128)}), f32[8,2,1,8]{3,1,2,0:T(2,128)S(1)}, u32[]{:S(2)}, u32[]{:S(2)}) async-start(f32[8,2,1,8]{3,1,2,0:T(2,128)} %bitcast.56), calls=%async_computation.3 | async-start | bytes 16384 | tf_op jit(solution)/shard_map/all_to_all | solution.py:139
  196.6 2.5 copy-start.9
  196.6 2.5 copy-start.11
  279.2 0.6 copy-start.10
Sparse Core Ops, SparseCore 0:
  10.1 56.0 all-gather.1
where the time goes:
time: 289 us; the launch traced here: 287 us
  other arithmetic  98.8 us (34%)
  loops' own time  53.6 us (19%)
  matrix products  38.8 us (13%)
  local copies, waits for them, and re-layouts  31.4 us (11%)
  waiting for transfers between devices  27.4 us (9%)
  starting transfers between devices  22.3 us (8%)
  between operations  14.3 us (5%)
    another operation x1, loops' own time, body(): lax.map(one_slot, (got_faces.reshape((slot_count,) + intersection_faces.s...  32.3 us
    reduce_sum x25, other arithmetic, correlate(): jnp.mean(magnitude, axis=(-2, -1), keepdims=True)  30.3 us
    convert_element_type x52, other arithmetic, dft_tables(): jnp.sin(angles).astype(jnp.bfloat16)  29.3 us
    another operation x1, loops' own time, body(): lax.map(coarse_one, (face_order // per_tile, partner_tiles, coarse_peaks))  21.4 us
    all_to_all x1, waiting for transfers between devices, body(): lax.all_to_all(parcel, 'tile', split_axis=0, concat_axis=0, tiled=True)  17.7 us
    dot_general x28, matrix products, spectrum(): jnp.einsum('...jky,jyl->...kl', segment_one, second_tables, preferred_ele...  13.9 us
    neg x26, other arithmetic, spectrum(): -sine_table  13.5 us
    dynamic_slice x16, local copies, waits for them, and re-layouts, body(): lax.map(coarse_one, (face_order // per_tile, partner_tiles, coarse_peaks))  10.2 us
  transfers between devices with their start and end apart: 6, of which 3 were waited for; matrix products, arithmetic and copies ran while one was open for 37% of the time, Pallas kernels for 0%

commit v1 on v0

--- a/solution.py
+++ b/solution.py
@@ -1,9 +1,17 @@
+import functools
+
 import jax
 import jax.numpy as jnp
+import ml_dtypes
+import numpy as np
 from jax import lax
+from jax.experimental import pallas as pl
+from jax.experimental.pallas import tpu as pltpu
 from jax.sharding import PartitionSpec as P
 
 TWO_PI = 6.283185307179586
+LANES = 128
+MESH = pl.DeviceIdType.MESH
 
 
 def from_behind(value, axis, steps):
@@ -93,7 +101,6 @@
     per_tile = face_dev // tile_dev
     windows = intersection_faces.shape[1]
     peak_count = face_peaks.shape[2]
-    coarse_side = coarse.shape[-1]
     tile_count = lax.axis_size("tile")
     capacity = max(2, (face_dev + tile_count - 1) // tile_count)
     slot_count = tile_count * capacity
@@ -107,13 +114,14 @@
     source = jnp.sum(jnp.where(slot_match, face_order[None, :], 0), axis=1)
     requests = jnp.where(filled, partner[source] + 1, 0).reshape(tile_count, capacity)
     own_real, own_imag = spectrum(intersection_faces)
-    parcel = jnp.where(
-        filled[:, None, None, None],
-        intersection_faces[source],
-        jnp.zeros_like(intersection_faces[source]),
-    )
+    parcel = jnp.einsum(
+        "sf,fwxy->swxy", slot_match.astype(jnp.bfloat16), intersection_faces,
+        preferred_element_type=jnp.float32,
+    ).astype(jnp.bfloat16)
     parcel = parcel.reshape((tile_count, capacity) + intersection_faces.shape[1:])
-    peak_marks = face_peaks[source].reshape((tile_count, capacity) + face_peaks.shape[1:])
+    peak_marks = jnp.sum(
+        jnp.where(slot_match[:, :, None, None], face_peaks[None], 0), axis=1
+    ).reshape((tile_count, capacity) + face_peaks.shape[1:])
     got_faces, got_marks, wanted_ids = (
         lax.all_to_all(parcel, "tile", split_axis=0, concat_axis=0, tiled=True),
         lax.all_to_all(peak_marks, "tile", split_axis=0, concat_axis=0, tiled=True),
@@ -146,29 +154,441 @@
     fine_scores = returned.reshape(slot_count, windows, peak_count)[slot_of]
     coarse_real, coarse_imag = spectrum(coarse)
     wanted_tile = target * tile_dev + partner // per_tile
-    empty_tiles = jnp.zeros((face_dev, coarse_side, coarse_side), jnp.bfloat16)
     shard_rows = lax.all_gather(coarse, "tile", axis=0, tiled=True)
     row_count = shard_rows.shape[0]
-    inside = (wanted_tile >= 0) & (wanted_tile < row_count)
-    selected = shard_rows[jnp.clip(wanted_tile, 0, row_count - 1)]
-    partner_tiles = jnp.where(inside[:, None, None], selected, empty_tiles)
-
     def coarse_one(packed):
-        tile_slot, other_tile, mark_in = packed
+        tile_slot, wanted, mark_in = packed
+        other_tile = lax.dynamic_index_in_dim(
+            shard_rows, jnp.clip(wanted, 0, row_count - 1), keepdims=False
+        )
         return correlate(
             (coarse_real[tile_slot], coarse_imag[tile_slot]), spectrum(other_tile), mark_in
         )
 
-    coarse_scores = lax.map(coarse_one, (face_order // per_tile, partner_tiles, coarse_peaks))
+    coarse_scores = lax.map(coarse_one, (face_order // per_tile, wanted_tile, coarse_peaks))
     lower_in = from_behind(lower_faces, "sec", 1)
     section_marks = section_peaks[:, None]
     section_scores = correlate(spectrum(upper_faces), spectrum(lower_in), section_marks)
     return (fine_scores, coarse_scores, section_scores)
 
 
+def np_tables(n):
+    index = np.arange(n)
+    angles = ((index[:, None] * index[None, :]) % n).astype(np.float32) * np.float32(TWO_PI / n)
+    return np.cos(angles), np.sin(angles)
+
+
+def split_tables(n, parts):
+    cosine, sine = np_tables(n)
+    rows = n // 2 // parts
+    slots = sine[: n // 2].copy()
+    slots[0] = cosine[n // 2]
+    first = np.concatenate(
+        [cosine[: n // 2].reshape(parts, rows, n), slots.reshape(parts, rows, n)], axis=1
+    ).reshape(n, n)
+    second = np.concatenate([cosine, sine], axis=1)
+    marks = np.zeros((parts, 2, n, 2 * (rows + 8)), np.float32)
+    for part in range(parts):
+        bins = list(range(part * rows, (part + 1) * rows))
+        weight = np.array([1.0 if k == 0 else 2.0 for k in bins] + [1.0 if part == 0 else 0.0] + [0.0] * 7)
+        bins = bins + [n // 2] * 8
+        c, s = cosine[bins].T * weight, sine[bins].T * weight
+        marks[part, 0] = np.concatenate([c, -s], axis=1)
+        marks[part, 1] = np.concatenate([s, c], axis=1)
+    return [bf16(first), bf16(second), bf16(marks)]
+
+
+def whole_tables(n):
+    cosine, sine = np_tables(n)
+    rows = n // 2 + 8
+    first = np.concatenate([cosine[:rows], sine[:rows]], axis=0)
+    weight = np.array([1.0] + [2.0] * (n // 2 - 1) + [1.0] + [0.0] * 7)
+    c, s = cosine[:rows].T * weight, sine[:rows].T * weight
+    marks = np.stack([np.concatenate([c, -s], axis=1), np.concatenate([s, c], axis=1)])
+    return [bf16(first), bf16(marks), np.tile(weight[:, None], (1, n)).astype(np.float32)]
+
+
+def bf16(table):
+    return table.astype(np.float32).astype(ml_dtypes.bfloat16)
+
+
+def hann(n):
+    x = np.arange(n, dtype=np.float32)
+    values = (0.5 - 0.5 * np.cos((x + np.float32(0.5)) * np.float32(TWO_PI / n))).astype(np.float32)
+    return [values[:, None], values[None, :]]
+
+
+def iota(shape, axis):
+    return lax.broadcasted_iota(jnp.int32, shape, axis)
+
+
+def mm(a, b):
+    return jnp.dot(a, b, preferred_element_type=jnp.float32)
+
+
+def pick(onehot, table):
+    return lax.dot_general(
+        onehot, table, (((0,), (0,)), ((), ())), preferred_element_type=jnp.float32
+    )
+
+
+def fold(value):
+    total = value[:, :LANES]
+    for start in range(LANES, value.shape[1], LANES):
+        total = total + value[:, start : start + LANES]
+    return total
+
+
+def windowed(image, column, row):
+    return (image.astype(jnp.float32) * column * row).astype(jnp.bfloat16)
+
+
+def cross(ar, ai, br, bi):
+    xr = ar * br + ai * bi
+    xi = ai * br - ar * bi
+    power = xr * xr + xi * xi
+    inverse = lax.rsqrt(jnp.maximum(power, 1e-37))
+    return xr, xi, inverse, power * inverse
+
+
+def to_row(column, shift):
+    shape = (column.shape[0], LANES)
+    here = iota(shape, 1) == iota(shape, 0) + shift
+    return jnp.sum(jnp.where(here, column, 0.0), axis=0, keepdims=True)
+
+
+def to_grid(rows, shift, count):
+    shape = (8, LANES)
+    kept = jnp.where(iota(shape, 1) // count == iota(shape, 0) + shift, rows, 0.0)
+    chosen = (iota((LANES, count), 0) % count == iota((LANES, count), 1)).astype(jnp.float32)
+    return jnp.dot(kept, chosen, precision=lax.Precision.HIGHEST, preferred_element_type=jnp.float32)
+
+
+def kernel(
+    T, NS,
+    ints, faces, coarse, upper, lower,
+    f_col, f_row, c_col, c_row, f_first, f_second, f_marks, c_first, c_second, c_marks,
+    s_first, s_marks, s_weight,
+    fine_out, coarse_out, section_out,
+    ints_all, ints_sm, low, f_send, f_all, c_send, c_all,
+    f_sr, f_si, c_sr, c_si, f_xr, f_xi, f_in, c_xr, c_xi, c_in,
+    f_a, f_cs, c_a, c_cs, f_sums, c_sums, f_msg, c_msg, f_tot, c_tot, f_it, c_it,
+    f_part, c_part, out_msg, out_all,
+    send_sems, recv_sems, low_sems, local_sem,
+):
+    me, sec = lax.axis_index("tile"), lax.axis_index("sec")
+    FD, TD = faces.shape[0], coarse.shape[0]
+    per_tile = FD // TD
+    PK = fine_out.shape[1]
+    pairs = T * FD
+    barrier = pltpu.get_barrier_semaphore()
+    for step in range(1, T):
+        pl.semaphore_signal(barrier, inc=1, device_id={"tile": lax.rem(me + step, T)}, device_id_type=MESH)
+
+    @pl.when(sec < NS - 1)
+    def _():
+        pl.semaphore_signal(barrier, inc=1, device_id={"sec": sec + 1}, device_id_type=MESH)
+
+    @pl.when(sec > 0)
+    def _():
+        pl.semaphore_signal(barrier, inc=1, device_id={"sec": sec - 1}, device_id_type=MESH)
+
+    def exchange(kind, step, source, landing):
+        peer = lax.rem(me + step, T)
+        return pltpu.make_async_remote_copy(
+            src_ref=source(peer), dst_ref=landing.at[me], send_sem=send_sems.at[kind, step],
+            recv_sem=recv_sems.at[kind, me], device_id={"tile": peer}, device_id_type=MESH,
+        )
+
+    def start(kind, source, landing):
+        for step in range(1, T):
+            exchange(kind, step, source, landing).start()
+
+    def arrive(kind, source, landing):
+        for step in range(1, T):
+            peer = lax.rem(me + step, T)
+            pltpu.make_async_remote_copy(
+                src_ref=source(peer), dst_ref=landing.at[peer], send_sem=send_sems.at[kind, step],
+                recv_sem=recv_sems.at[kind, peer], device_id={"tile": peer}, device_id_type=MESH,
+            ).wait_recv()
+
+    def sent(kind, source, landing):
+        for step in range(1, T):
+            exchange(kind, step, source, landing).wait_send()
+
+    def lower_copy():
+        return pltpu.make_async_remote_copy(
+            src_ref=lower, dst_ref=low, send_sem=low_sems.at[0], recv_sem=low_sems.at[1],
+            device_id={"sec": lax.rem(sec + 1, NS)}, device_id_type=MESH,
+        )
+
+    def first_step(images, col, row, table, out, count):
+        n = images.shape[-1]
+        for which in range(count):
+            got = mm(table[...], windowed(images[which], col[...], row[...]))
+            out[:, which] = got.astype(jnp.bfloat16).reshape(T, n // T, n)
+
+    first_step(faces, f_col, f_row, f_first, f_send, FD)
+
+    @pl.when((sec > 0) & (sec < NS - 1))
+    def _():
+        pl.semaphore_wait(barrier, T + 1)
+
+    @pl.when((sec == 0) | (sec == NS - 1))
+    def _():
+        pl.semaphore_wait(barrier, T - 1 + (1 if NS > 1 else 0))
+
+    sources = [lambda peer: ints, lambda peer: f_send.at[peer], lambda peer: c_send.at[peer],
+               lambda peer: f_msg, lambda peer: c_msg, lambda peer: out_msg.at[peer]]
+    landings = [ints_all, f_all, c_all, f_tot, c_tot, out_all]
+    start(0, sources[0], landings[0])
+    start(1, sources[1], landings[1])
+
+    @pl.when(sec < NS - 1)
+    def _():
+        lower_copy().start()
+
+    first_step(coarse, c_col, c_row, c_first, c_send, TD)
+    start(2, sources[2], landings[2])
+    ints_all[me] = ints[...]
+    f_all[me] = f_send[me]
+    c_all[me] = c_send[me]
+
+    arrive(0, sources[0], landings[0])
+    to_scalar = pltpu.make_async_copy(ints_all, ints_sm, local_sem)
+    to_scalar.start()
+
+    def tables_of(row, n, second, marks, a, cs, at):
+        onehot = jnp.where(iota((n, LANES), 0) == row, 1.0, 0.0).astype(jnp.bfloat16)
+        half = FD * PK
+        width = 2 * n
+        cs[pl.ds(at, FD)] = pick(onehot, second)[half:].reshape(FD, PK, width)
+        for side in range(2):
+            a[pl.ds(at, FD), side * PK : (side + 1) * PK, :] = pick(onehot, marks[side])[:half].reshape(FD, PK, -1)
+
+    def peaks_from(j, _):
+        rows = ints_all[j]
+        tables_of(rows[0:1], f_row.shape[1], f_second[...], f_marks[me], f_a, f_cs, j * FD)
+        tables_of(rows[1:2], c_row.shape[1], c_second[...], c_marks[me], c_a, c_cs, j * FD)
+        return 0
+
+    lax.fori_loop(0, T, peaks_from, 0)
+
+    @pl.when(sec > 0)
+    def _():
+        lower_copy().wait_recv()
+
+    @pl.when(sec == 0)
+    def _():
+        low[...] = jnp.zeros_like(low)
+
+    n = f_row.shape[1]
+    rows_s = n // 2 + 8
+
+    def spectrum_s(image):
+        got = mm(s_first[...], windowed(image, f_col[...], f_row[...])).astype(jnp.bfloat16)
+        both = mm(got, f_second[...])
+        p, q = both[:rows_s], both[rows_s:]
+        return p[:, :n] - q[:, n:], -(p[:, n:] + q[:, :n])
+
+    onehot = jnp.where(iota((n, LANES), 0) == ints[3:4], 1.0, 0.0).astype(jnp.bfloat16)
+    cs_s = pick(onehot, f_second[...])[TD * PK : 2 * TD * PK]
+    a_s = [pick(onehot, s_marks[side])[: TD * PK] for side in range(2)]
+    columns = []
+    for which in range(TD):
+        ar, ai = spectrum_s(upper[which])
+        br, bi = spectrum_s(low[which])
+        xr, xi, inverse, size = cross(ar, ai, br, bi)
+        total = jnp.sum(jnp.sum(size * s_weight[...], axis=0, keepdims=True), axis=1, keepdims=True)
+        scale = jnp.minimum(inverse, 1.0 / (total * (0.05 / (n * n)) + 1e-6))
+        unit = jnp.concatenate([xr * scale, xi * scale], axis=0).astype(jnp.bfloat16)
+        at = slice(which * PK, (which + 1) * PK)
+        fr = mm(a_s[0][at].astype(jnp.bfloat16), unit)
+        fi = mm(a_s[1][at].astype(jnp.bfloat16), unit)
+        columns.append(jnp.sum(fr * cs_s[at, :n] - fi * cs_s[at, n:], axis=1, keepdims=True))
+    row = to_row(jnp.concatenate(columns, axis=0), 0)
+    section_out[...] = to_grid(jnp.broadcast_to(row, (8, LANES)), 0, PK)[:TD] * (1.0 / n)
+
+    to_scalar.wait()
+
+    def second_step(block, n, second, sr, si, groups):
+        rows = n // 2 // T
+        per = T // groups
+        images = block.shape[1]
+        for group in range(groups):
+            x = block[group * per : (group + 1) * per].reshape(per * images * 2 * rows, n)
+            both = mm(x, second[...]).reshape(per * images, 2 * rows, 2 * n)
+            p, q = both[:, :rows], both[:, rows:]
+            special = (iota((1, rows, 1), 1) == 0) & (me == 0)
+            at = slice(group * per * images, (group + 1) * per * images)
+            sr[at, :rows, :] = p[:, :, :n] - jnp.where(special, 0.0, q[:, :, n:])
+            si[at, :rows, :] = -(p[:, :, n:] + jnp.where(special, 0.0, q[:, :, :n]))
+            sr[at, rows:, :] = q[:, :8, :n]
+            si[at, rows:, :] = -q[:, :8, n:]
+
+    def weights(rows, n):
+        at = iota((rows + 8, n), 0)
+        main = jnp.where((at == 0) & (me == 0), 1.0, 2.0)
+        extra = jnp.where((at == rows) & (me == 0), 1.0, 0.0)
+        return jnp.where(at < rows, main, extra)
+
+    def cross_all(n, sr, si, xr, xi, inv, sums, own_of, other_of, msg):
+        w = weights(n // 2 // T, n)
+
+        def one(p, _):
+            own, other = own_of(p), other_of(p)
+            vr, vi, inverse, size = cross(sr[own], si[own], sr[other], si[other])
+            xr[p], xi[p], inv[p] = vr, vi, inverse
+            sums[pl.ds(p, 1), :] = fold(jnp.sum(size * w, axis=0, keepdims=True))
+            return 0
+
+        lax.fori_loop(0, pairs, one, 0, unroll=4)
+        total = jnp.sum(sums[...], axis=1, keepdims=True)
+        msg[...] = jnp.broadcast_to(to_row(total, 0), msg.shape)
+
+    def score_all(n, tot, it, xr, xi, inv, a, cs, part):
+        row = jnp.sum(tot[...], axis=0)[0:1]
+        limit = 1.0 / (row * (0.05 / (n * n)) + 1e-6)
+        shape = (pairs, LANES)
+        column = jnp.sum(jnp.where(iota(shape, 1) == iota(shape, 0), limit, 0.0), axis=1, keepdims=True)
+        it[...] = jnp.broadcast_to(column, it.shape)
+
+        def one(p, _):
+            scale = jnp.minimum(inv[p], it[pl.ds(p, 1), :])
+            unit = jnp.concatenate([xr[p] * scale, xi[p] * scale], axis=0).astype(jnp.bfloat16)
+            got = mm(a[p].astype(jnp.bfloat16), unit)
+            table = cs[p]
+            part[p] = fold(got[:PK] * table[:, :n] - got[PK:] * table[:, n:])
+            return 0
+
+        lax.fori_loop(0, pairs, one, 0, unroll=4)
+
+    NF, NC = f_row.shape[1], c_row.shape[1]
+    arrive(1, sources[1], landings[1])
+    second_step(f_all, NF, f_second, f_sr, f_si, 2)
+    cross_all(
+        NF, f_sr, f_si, f_xr, f_xi, f_in, f_sums, lambda p: p,
+        lambda p: ints_sm[p // FD, 2, p % FD] * FD + ints_sm[p // FD, 2, FD + p % FD], f_msg,
+    )
+    start(3, sources[3], landings[3])
+    f_tot[me] = f_msg[...]
+    arrive(2, sources[2], landings[2])
+    second_step(c_all, NC, c_second, c_sr, c_si, 2)
+    cross_all(
+        NC, c_sr, c_si, c_xr, c_xi, c_in, c_sums, lambda p: p // per_tile,
+        lambda p: ints_sm[p // FD, 2, p % FD] * TD + ints_sm[p // FD, 2, FD + p % FD] // per_tile, c_msg,
+    )
+    start(4, sources[4], landings[4])
+    c_tot[me] = c_msg[...]
+    arrive(3, sources[3], landings[3])
+    score_all(NF, f_tot, f_it, f_xr, f_xi, f_in, f_a, f_cs, f_part)
+    arrive(4, sources[4], landings[4])
+    score_all(NC, c_tot, c_it, c_xr, c_xi, c_in, c_a, c_cs, c_part)
+
+    def gather(j, _):
+        def column(part):
+            block = part[pl.ds(j * FD, FD)].reshape(FD * PK, LANES)
+            return jnp.sum(block, axis=1, keepdims=True)
+
+        row = to_row(column(c_part), 0) + to_row(column(f_part), FD * PK)
+        out_msg[j] = jnp.broadcast_to(row, (8, LANES))
+        return 0
+
+    lax.fori_loop(0, T, gather, 0)
+    start(5, sources[5], landings[5])
+    out_all[me] = out_msg[me]
+    for kind in range(5):
+        sent(kind, sources[kind], landings[kind])
+
+    @pl.when(sec < NS - 1)
+    def _():
+        lower_copy().wait_send()
+
+    arrive(5, sources[5], landings[5])
+    total = jnp.sum(out_all[...], axis=0)
+    coarse_out[...] = to_grid(total, 0, PK) * (1.0 / NC)
+    fine_out[...] = to_grid(total, FD, PK) * (1.0 / NF)
+    sent(5, sources[5], landings[5])
+
+
+def split_body(
+    T, NS, intersection_faces, destination, partner, face_peaks, coarse, coarse_peaks,
+    upper_faces, lower_faces, section_peaks,
+):
+    FD, TD, PK = intersection_faces.shape[0], coarse.shape[0], face_peaks.shape[2]
+    NF, NC = intersection_faces.shape[-1], coarse.shape[-1]
+    pairs = T * FD
+
+    def line(*parts):
+        flat = jnp.concatenate([part.reshape(-1) for part in parts])
+        return jnp.pad(flat, (0, LANES - flat.shape[0]))
+
+    ints = jnp.stack([
+        line(face_peaks[:, 0], face_peaks[:, 1]),
+        line(coarse_peaks[:, 0], coarse_peaks[:, 1]),
+        line(destination, partner),
+        line(section_peaks[:, 0], section_peaks[:, 1]),
+    ] + [jnp.zeros((LANES,), jnp.int32)] * 4)
+    operands = [
+        ints, intersection_faces.reshape(FD, NF, NF), coarse,
+        upper_faces.reshape(TD, NF, NF), lower_faces.reshape(TD, NF, NF),
+    ] + [jnp.asarray(t) for t in (
+        hann(NF) + hann(NC) + split_tables(NF, T) + split_tables(NC, T) + whole_tables(NF)
+    )]
+    fr, cr = NF // 2 // T + 8, NC // 2 // T + 8
+    f32 = jnp.float32
+    V = pltpu.VMEM
+    scratch = [
+        V((T, 8, LANES), jnp.int32), pltpu.SMEM((T, 8, LANES), jnp.int32),
+        V((TD, NF, NF), jnp.bfloat16),
+        V((T, FD, NF // T, NF), jnp.bfloat16), V((T, FD, NF // T, NF), jnp.bfloat16),
+        V((T, TD, NC // T, NC), jnp.bfloat16), V((T, TD, NC // T, NC), jnp.bfloat16),
+        V((pairs, fr, NF), f32), V((pairs, fr, NF), f32),
+        V((T * TD, cr, NC), f32), V((T * TD, cr, NC), f32),
+    ] + [V((pairs, fr, NF), f32)] * 3 + [V((pairs, cr, NC), f32)] * 3 + [
+        V((pairs, 2 * PK, 2 * fr), f32), V((pairs, PK, 2 * NF), f32),
+        V((pairs, 2 * PK, 2 * cr), f32), V((pairs, PK, 2 * NC), f32),
+        V((pairs, LANES), f32), V((pairs, LANES), f32),
+        V((8, LANES), f32), V((8, LANES), f32),
+        V((T, 8, LANES), f32), V((T, 8, LANES), f32),
+        V((pairs, NF), f32), V((pairs, NC), f32),
+        V((pairs, PK, LANES), f32), V((pairs, PK, LANES), f32),
+        V((T, 8, LANES), f32), V((T, 8, LANES), f32),
+        pltpu.SemaphoreType.DMA((6, T)), pltpu.SemaphoreType.DMA((6, T)),
+        pltpu.SemaphoreType.DMA((2,)), pltpu.SemaphoreType.DMA,
+    ]
+    fine, coarse_scores, section = pl.pallas_call(
+        functools.partial(kernel, T, NS),
+        out_shape=(
+            jax.ShapeDtypeStruct((FD, PK), f32), jax.ShapeDtypeStruct((FD, PK), f32),
+            jax.ShapeDtypeStruct((TD, PK), f32),
+        ),
+        in_specs=[pl.BlockSpec(memory_space=pltpu.VMEM)] * len(operands),
+        out_specs=(pl.BlockSpec(memory_space=pltpu.VMEM),) * 3,
+        scratch_shapes=scratch,
+        compiler_params=pltpu.CompilerParams(
+            collective_id=0, has_side_effects=True, vmem_limit_bytes=44 * 1024 * 1024
+        ),
+    )(*operands)
+    return fine.reshape(FD, 1, PK), coarse_scores, section.reshape(TD, 1, PK)
+
+
+def choose(T, NS, *args):
+    faces, coarse, peaks = args[0], args[4], args[3]
+    fits = (
+        faces.shape[1] == 1
+        and peaks.shape[2] == 8
+        and faces.shape[0] == 8
+        and faces.shape[-1] // 2 % (8 * T) == 0
+        and coarse.shape[-1] // 2 % (8 * T) == 0
+        and T * faces.shape[0] <= LANES
+    )
+    return split_body(T, NS, *args) if fits else body(*args)
+
+
 def solution(mesh):
     return jax.shard_map(
-        body,
+        functools.partial(choose, mesh.shape["tile"], mesh.shape["sec"]),
         mesh=mesh,
         in_specs=(
             P(("sec", "tile"), None, None, None),

time: 289 us -> 52 us (0.18)
  other arithmetic: 98.8 us -> 0.98 us
  loops' own time: 53.6 us -> 0 us
  matrix products: 38.8 us -> 0 us
  Pallas kernels: 0 us -> 33.2 us
  waiting for transfers between devices: 27.4 us -> 0 us
  starting transfers between devices: 22.3 us -> 0 us
  local copies, waits for them, and re-layouts: 31.4 us -> 16.4 us
  between operations: 14.3 us -> 0.72 us
    another operation x2 -> x0, loops' own time: 53.6 us -> none  [the longest x1 32.3 us: body(): lax.map(one_slot, (got_faces.reshape((slot_count,) + intersection_faces.s...]
    dot_general x128 -> x0, matrix products: 38.8 us -> none  [the longest x28 13.9 us: spectrum(): jnp.einsum('...jky,jyl->...kl', segment_one, second_tables, preferred_ele...]
    pallas_call x0 -> x1, Pallas kernels: none -> 33.2 us  [split_body(): pl.pallas_call(functools.partial(kernel, T, NS), out_shape=(jax.ShapeDtyp...]
    reduce_sum x27 -> x0, other arithmetic: 31.3 us -> none  [the longest x25 30.3 us: correlate(): jnp.mean(magnitude, axis=(-2, -1), keepdims=True)]
    convert_element_type x52 -> x0, other arithmetic: 29.3 us -> none  [dft_tables(): jnp.sin(angles).astype(jnp.bfloat16)]
    all_to_all x4 -> x0, waiting for transfers between devices: 26.7 us -> none  [the longest x1 17.7 us: body(): lax.all_to_all(parcel, 'tile', split_axis=0, concat_axis=0, tiled=True)]
    all_to_all x4 -> x0, starting transfers between devices: 20.2 us -> none  [the longest x1 7.28 us: body(): lax.all_to_all(requests, 'tile', split_axis=0, concat_axis=0, tiled=True)]
    dynamic_slice x48 -> x0, local copies, waits for them, and re-layouts: 19.6 us -> none  [the longest x16 10.2 us: body(): lax.map(coarse_one, (face_order // per_tile, partner_tiles, coarse_peaks))]
  transfers between devices with their start and end apart: 6 -> 0, of which waited for: 3 -> 0; matrix products, arithmetic and copies ran while one was open for 37% -> 0% of each run, Pallas kernels for 0% -> 0%
where the time goes in v1:
time: 52 us; the launch traced here: 51.3 us
  Pallas kernels  33.2 us (64%)
  local copies, waits for them, and re-layouts  16.4 us (32%)
  other arithmetic  0.98 us (2%)
  between operations  0.72 us (1%)
    pallas_call x1, Pallas kernels, split_body(): pl.pallas_call(functools.partial(kernel, T, NS), out_shape=(jax.ShapeDtyp...  33.2 us
    unnamed x37, local copies, waits for them, and re-layouts  14.3 us

profile of v1, /device:TPU:0, one launch (start us, length us, event | category | flops | bytes accessed | tf_op | source)
XLA Modules:
  0.0 51.3 jit_solution(12094443336696959057)
XLA Ops:
  0.6 0.0 copy-start.15
  0.6 0.0 copy-start.8
  0.7 0.8 %slice_reduce_fusion.1 = (s32[8,8]{1,0:T(8,128)S(1)}, s32[8,8]{1,0:T(8,128)S(1)}, s32[8,8]{1,0:T(8,128)S(1)}, s32[8,8]{1,0:T(8,128)S(1)}) fusion(s32[8,2,8]{2,1,0:T(2,128)} %param.27, s32[8,2,8]{2,1,0:T(2,128)} %param.25), kind=kLoop, calls=%fused_computation.1 | loop fusion | bytes 2048 | tf_op jit(solution)/shard_map/slice | solution.py:528
  1.5 0.0 copy-start.12
  1.5 0.1 reshape_squeeze.20
  1.6 0.1 reshape_squeeze.21
  1.7 0.1 add_bitcast_fusion.1
  1.7 0.1 reshape_squeeze.18
  1.8 0.1 reshape_squeeze.19
  1.9 0.1 add_bitcast_fusion
  2.0 0.8 %slice_reduce_fusion.5 = (s32[2,8]{1,0:T(2,128)S(1)}, s32[2,8]{1,0:T(2,128)S(1)}) fusion(s32[2,2,8]{2,1,0:T(2,128)} %param.30), kind=kLoop, calls=%fused_computation.5 | loop fusion | bytes 256 | tf_op jit(solution)/shard_map/slice | solution.py:530
  2.8 0.1 reshape_squeeze.22
  2.8 0.1 reshape_squeeze.23
  2.9 0.1 pad_add_fusion.1
  3.0 0.7 %pad_add_fusion = s32[16]{0:T(128)S(1)} fusion(s32[8]{0:T(128)} %param.24, s32[8]{0:T(128)} %bitcast.23), kind=kLoop, calls=%fused_computation.8 | loop fusion | flops 16 | bytes 128 | tf_op jit(solution)/shard_map/concatenate | solution.py:523
  3.8 0.0 copy-start.16
  3.8 0.0 copy-done.15
  3.8 0.0 copy-done.8
  3.8 0.0 copy-done.12
  3.8 0.6 %copy-done.16 = f32[1,128]{1,0:T(1,128)S(1)} copy-done((f32[1,128]{1,0:T(1,128)S(1)}, f32[1,128]{1,0:T(1,128)}, u32[]{:S(2)}) %copy-start.16) | copy-done | bytes 536
  4.4 0.0 copy-start
  4.4 1.2 %copy-done = bf16[8,2,256,48]{3,2,1,0:T(8,128)(2,1)S(1)} copy-done((bf16[8,2,256,48]{3,2,1,0:T(8,128)(2,1)S(1)}, bf16[8,2,256,48]{3,2,1,0:T(8,128)(2,1)}, u32[]{:S(2)}) %copy-start) | copy-done | bytes 393240
  5.7 0.0 copy-start.1
  5.7 1.0 %copy-done.1 = bf16[8,2,128,32]{3,2,1,0:T(8,128)(2,1)S(1)} copy-done((bf16[8,2,128,32]{3,2,1,0:T(8,128)(2,1)S(1)}, bf16[8,2,128,32]{3,2,1,0:T(8,128)(2,1)}, u32[]{:S(2)}) %copy-start.1) | copy-done | bytes 131096
  6.7 0.0 copy-start.2
  6.7 0.9 %copy-done.2 = bf16[8,1,128,128]{3,2,1,0:T(8,128)(2,1)S(1)} copy-done((bf16[8,1,128,128]{3,2,1,0:T(8,128)(2,1)S(1)}, bf16[8,1,128,128]{3,2,1,0:T(8,128)(2,1)}, u32[]{:S(2)}) %copy-start.2) | copy-done | bytes 262168
  7.7 0.0 copy-start.3
  7.7 0.9 %copy-done.3 = bf16[2,256,256]{2,1,0:T(8,128)(2,1)S(1)} copy-done((bf16[2,256,256]{2,1,0:T(8,128)(2,1)S(1)}, bf16[2,256,256]{2,1,0:T(8,128)(2,1)}, u32[]{:S(2)}) %copy-start.3) | copy-done | bytes 262168
  8.6 0.0 copy-start.4
  8.6 0.9 %copy-done.4 = bf16[256,512]{1,0:T(8,128)(2,1)S(1)} copy-done((bf16[256,512]{1,0:T(8,128)(2,1)S(1)}, bf16[256,512]{1,0:T(8,128)(2,1)}, u32[]{:S(2)}) %copy-start.4) | copy-done | bytes 262168
  9.6 0.0 copy-start.5
  9.6 0.9 %copy-done.5 = f32[256,1]{1,0:T(8,128)S(1)} copy-done((f32[256,1]{1,0:T(8,128)S(1)}, f32[256,1]{1,0:T(8,128)}, u32[]{:S(2)}) %copy-start.5) | copy-done | bytes 1048
  10.5 0.0 copy-start.6
  10.5 0.9 %copy-done.6 = bf16[256,256]{1,0:T(8,128)(2,1)S(1)} copy-done((bf16[256,256]{1,0:T(8,128)(2,1)S(1)}, bf16[256,256]{1,0:T(8,128)(2,1)}, u32[]{:S(2)}) %copy-start.6) | copy-done | bytes 131096
  11.4 0.0 copy-start.7
  11.4 0.9 %copy-done.7 = bf16[2,128,144]{2,1,0:T(8,128)(2,1)S(1)} copy-done((bf16[2,128,144]{2,1,0:T(8,128)(2,1)S(1)}, bf16[2,128,144]{2,1,0:T(8,128)(2,1)}, u32[]{:S(2)}) %copy-start.7) | copy-done | bytes 73752
  12.3 0.0 copy-start.9
  12.3 0.8 %copy-done.9 = bf16[2,1,128,128]{3,2,1,0:T(8,128)(2,1)S(1)} copy-done((bf16[2,1,128,128]{3,2,1,0:T(8,128)(2,1)S(1)}, bf16[2,1,128,128]{3,2,1,0:T(8,128)(2,1)}, u32[]{:S(2)}) %copy-start.9) | copy-done | bytes 65560
  13.1 0.0 copy-start.10
  13.1 0.8 %copy-done.10 = f32[128,1]{1,0:T(8,128)S(1)} copy-done((f32[128,1]{1,0:T(8,128)S(1)}, f32[128,1]{1,0:T(8,128)}, u32[]{:S(2)}) %copy-start.10) | copy-done | bytes 536
  13.9 0.0 copy-start.11
  13.9 0.8 %copy-done.11 = bf16[128,256]{1,0:T(8,128)(2,1)S(1)} copy-done((bf16[128,256]{1,0:T(8,128)(2,1)S(1)}, bf16[128,256]{1,0:T(8,128)(2,1)}, u32[]{:S(2)}) %copy-start.11) | copy-done | bytes 65560
  14.8 0.0 copy-start.13
  14.8 0.8 %copy-done.13 = f32[72,128]{1,0:T(8,128)S(1)} copy-done((f32[72,128]{1,0:T(8,128)S(1)}, f32[72,128]{1,0:T(8,128)}, u32[]{:S(2)}) %copy-start.13) | copy-done | bytes 36888
  15.6 0.0 copy-start.14
  15.6 0.8 %copy-done.14 = bf16[128,128]{1,0:T(8,128)(2,1)S(1)} copy-done((bf16[128,128]{1,0:T(8,128)(2,1)S(1)}, bf16[128,128]{1,0:T(8,128)(2,1)}, u32[]{:S(2)}) %copy-start.14) | copy-done | bytes 32792
  16.3 33.2 %shard_map.229 = (f32[8,8]{1,0:T(8,128)S(1)}, f32[8,8]{1,0:T(8,128)S(1)}, f32[2,8]{1,0:T(2,128)S(1)}) custom-call(s32[8,128]{1,0:T(8,128)S(1)} %stack.23.ints, bf16[8,128,128]{2,1,0:T(8,128)(2,1)S(1)} %bitcast.18, bf16[2,256,256]{2,1,0:T(8,128)(2,1)S(1)} %copy-done.3, bf16[2,128,128]{2,1,0:T(8,128)(2,1)S(1)} %bitcast.19, bf16[2,128,128]{2,1,0:T(8,128)(2,1)S(1)} %bitcast.20, ...), custom_call_target="tpu_custom_call" | custom-call | tf_op jit(solution)/shard_map/pallas_call | solution.py:560
  49.6 0.6 %copy.32 = f32[8,1,8]{2,1,0:T(1,128)} copy(f32[8,1,8]{2,1,0:T(1,128)S(1)} %bitcast.21) | data formatting | bytes 512
  50.2 0.6 %copy.33 = f32[8,8]{1,0:T(8,128)} copy(f32[8,8]{1,0:T(8,128)S(1)} %get-tuple-element.29) | data formatting | bytes 512
  50.8 0.6 %copy.34 = f32[2,1,8]{2,1,0:T(1,128)} copy(f32[2,1,8]{2,1,0:T(1,128)S(1)} %bitcast.22) | data formatting | bytes 128
  (3 shorter events, 0.0 us)
Async XLA Ops:
  0.6 3.2 %copy-start.15 = (f32[1,256]{1,0:T(1,128)S(1)}, f32[1,256]{1,0:T(1,128)}, u32[]{:S(2)}) copy-start(f32[1,256]{1,0:T(1,128)} %constant.32.clone.c_row) | copy-start | bytes 3076
  0.6 3.2 %copy-start.8 = (bf16[2,1,128,128]{3,2,1,0:T(8,128)(2,1)S(1)}, bf16[2,1,128,128]{3,2,1,0:T(8,128)(2,1)}, u32[]{:S(2)}) copy-start(bf16[2,1,128,128]{3,2,1,0:T(8,128)(2,1)} %param.28) | copy-start | bytes 196612
  1.5 2.3 %copy-start.12 = (bf16[144,128]{1,0:T(8,128)(2,1)S(1)}, bf16[144,128]{1,0:T(8,128)(2,1)}, u32[]{:S(2)}) copy-start(bf16[144,128]{1,0:T(8,128)(2,1)} %constant.39.clone.s_first) | copy-start | bytes 110596
  3.8 0.7 %copy-start.16 = (f32[1,128]{1,0:T(1,128)S(1)}, f32[1,128]{1,0:T(1,128)}, u32[]{:S(2)}) copy-start(f32[1,128]{1,0:T(1,128)} %constant.30.clone.f_row) | copy-start | bytes 1540
  4.4 1.2 %copy-start = (bf16[8,2,256,48]{3,2,1,0:T(8,128)(2,1)S(1)}, bf16[8,2,256,48]{3,2,1,0:T(8,128)(2,1)}, u32[]{:S(2)}) copy-start(bf16[8,2,256,48]{3,2,1,0:T(8,128)(2,1)} %constant.38.clone.c_marks) | copy-start | bytes 1179652
  5.7 1.0 %copy-start.1 = (bf16[8,2,128,32]{3,2,1,0:T(8,128)(2,1)S(1)}, bf16[8,2,128,32]{3,2,1,0:T(8,128)(2,1)}, u32[]{:S(2)}) copy-start(bf16[8,2,128,32]{3,2,1,0:T(8,128)(2,1)} %constant.35.clone.f_marks) | copy-start | bytes 393220
  6.7 0.9 %copy-start.2 = (bf16[8,1,128,128]{3,2,1,0:T(8,128)(2,1)S(1)}, bf16[8,1,128,128]{3,2,1,0:T(8,128)(2,1)}, u32[]{:S(2)}) copy-start(bf16[8,1,128,128]{3,2,1,0:T(8,128)(2,1)} %param.22) | copy-start | bytes 786436
  7.7 0.9 %copy-start.3 = (bf16[2,256,256]{2,1,0:T(8,128)(2,1)S(1)}, bf16[2,256,256]{2,1,0:T(8,128)(2,1)}, u32[]{:S(2)}) copy-start(bf16[2,256,256]{2,1,0:T(8,128)(2,1)} %coarse.1) | copy-start | bytes 786436
  8.6 0.9 %copy-start.4 = (bf16[256,512]{1,0:T(8,128)(2,1)S(1)}, bf16[256,512]{1,0:T(8,128)(2,1)}, u32[]{:S(2)}) copy-start(bf16[256,512]{1,0:T(8,128)(2,1)} %constant.37.clone.c_second) | copy-start | bytes 786436
  9.6 0.9 %copy-start.5 = (f32[256,1]{1,0:T(8,128)S(1)}, f32[256,1]{1,0:T(8,128)}, u32[]{:S(2)}) copy-start(f32[256,1]{1,0:T(8,128)} %constant.31.clone.c_col) | copy-start | bytes 3076
  10.5 0.9 %copy-start.6 = (bf16[256,256]{1,0:T(8,128)(2,1)S(1)}, bf16[256,256]{1,0:T(8,128)(2,1)}, u32[]{:S(2)}) copy-start(bf16[256,256]{1,0:T(8,128)(2,1)} %constant.36.clone.c_first) | copy-start | bytes 393220
  11.4 0.9 %copy-start.7 = (bf16[2,128,144]{2,1,0:T(8,128)(2,1)S(1)}, bf16[2,128,144]{2,1,0:T(8,128)(2,1)}, u32[]{:S(2)}) copy-start(bf16[2,128,144]{2,1,0:T(8,128)(2,1)} %constant.40.clone.s_marks) | copy-start | bytes 221188
  12.3 0.8 %copy-start.9 = (bf16[2,1,128,128]{3,2,1,0:T(8,128)(2,1)S(1)}, bf16[2,1,128,128]{3,2,1,0:T(8,128)(2,1)}, u32[]{:S(2)}) copy-start(bf16[2,1,128,128]{3,2,1,0:T(8,128)(2,1)} %param.29) | copy-start | bytes 196612
  13.1 0.8 %copy-start.10 = (f32[128,1]{1,0:T(8,128)S(1)}, f32[128,1]{1,0:T(8,128)}, u32[]{:S(2)}) copy-start(f32[128,1]{1,0:T(8,128)} %constant.13.clone.f_col) | copy-start | bytes 1540
  13.9 0.8 %copy-start.11 = (bf16[128,256]{1,0:T(8,128)(2,1)S(1)}, bf16[128,256]{1,0:T(8,128)(2,1)}, u32[]{:S(2)}) copy-start(bf16[128,256]{1,0:T(8,128)(2,1)} %constant.34.clone.f_second) | copy-start | bytes 196612
  14.8 0.8 %copy-start.13 = (f32[72,128]{1,0:T(8,128)S(1)}, f32[72,128]{1,0:T(8,128)}, u32[]{:S(2)}) copy-start(f32[72,128]{1,0:T(8,128)} %constant.41.clone.s_weight) | copy-start | bytes 110596
  15.6 0.8 %copy-start.14 = (bf16[128,128]{1,0:T(8,128)(2,1)S(1)}, bf16[128,128]{1,0:T(8,128)(2,1)}, u32[]{:S(2)}) copy-start(bf16[128,128]{1,0:T(8,128)(2,1)} %constant.33.clone.f_first) | copy-start | bytes 98308

commit v2 on v1

--- a/solution.py
+++ b/solution.py
@@ -265,18 +265,37 @@
 
 
 def kernel(
-    T, NS,
-    ints, faces, coarse, upper, lower,
-    f_col, f_row, c_col, c_row, f_first, f_second, f_marks, c_first, c_second, c_marks,
-    s_first, s_marks, s_weight,
+    T, NS, h_dest, h_part, h_fp, h_cp, h_sp, h_faces, h_coarse, h_upper, lower,
+    h_f_col, h_f_row, h_c_col, h_c_row, h_f_first, h_f_second, h_f_marks,
+    h_c_first, h_c_second, h_c_marks, h_s_first, h_s_marks, h_s_weight,
     fine_out, coarse_out, section_out,
-    ints_all, ints_sm, low, f_send, f_all, c_send, c_all,
+    dest, part, fp, cp, sp, faces, coarse, upper, f_col, f_row, c_col, c_row,
+    f_first, f_second, f_marks, c_first, c_second, c_marks, s_first, s_marks, s_weight,
+    load_sems, ints, ints_all, ints_sm, low, f_send, f_all, c_send, c_all,
     f_sr, f_si, c_sr, c_si, f_xr, f_xi, f_in, c_xr, c_xi, c_in,
     f_a, f_cs, c_a, c_cs, f_sums, c_sums, f_msg, c_msg, f_tot, c_tot, f_it, c_it,
     f_part, c_part, out_msg, out_all,
     send_sems, recv_sems, low_sems, local_sem,
 ):
     me, sec = lax.axis_index("tile"), lax.axis_index("sec")
+    loads = [
+        pltpu.make_async_copy(source, target, load_sems.at[index])
+        for index, (source, target) in enumerate([
+            (h_f_col, f_col), (h_f_row, f_row), (h_f_first, f_first), (h_faces, faces),
+            (h_dest, dest), (h_part, part), (h_fp, fp), (h_cp, cp), (h_sp, sp),
+            (h_c_col, c_col), (h_c_row, c_row), (h_c_first, c_first), (h_coarse, coarse),
+            (h_f_second, f_second), (h_f_marks.at[me], f_marks),
+            (h_c_second, c_second), (h_c_marks.at[me], c_marks),
+            (h_upper, upper), (h_s_first, s_first), (h_s_marks, s_marks), (h_s_weight, s_weight),
+        ])
+    ]
+    for load in loads:
+        load.start()
+
+    def loaded(low_at, high_at):
+        for load in loads[low_at:high_at]:
+            load.wait()
+
     FD, TD = faces.shape[0], coarse.shape[0]
     per_tile = FD // TD
     PK = fine_out.shape[1]
@@ -328,6 +347,25 @@
             got = mm(table[...], windowed(images[which], col[...], row[...]))
             out[:, which] = got.astype(jnp.bfloat16).reshape(T, n // T, n)
 
+    def lanes_of(grid, shift):
+        count, width = grid.shape
+        chosen = iota((width, LANES), 1) % width == iota((width, LANES), 0)
+        spread = mm(grid.astype(jnp.float32).astype(jnp.bfloat16), chosen.astype(jnp.float32).astype(jnp.bfloat16))
+        shape = (count, LANES)
+        kept = iota(shape, 1) // width == iota(shape, 0) + shift
+        return jnp.sum(jnp.where(kept, spread, 0.0), axis=0, keepdims=True)
+
+    loaded(4, 9)
+    lines = [
+        lanes_of(fp[:, 0, :], 0) + lanes_of(fp[:, 1, :], FD),
+        lanes_of(cp[:, 0, :], 0) + lanes_of(cp[:, 1, :], FD),
+        lanes_of(sp[:, 0, :], 0) + lanes_of(sp[:, 1, :], TD),
+    ]
+    lines = jnp.concatenate(lines + [jnp.zeros((5, LANES), jnp.float32)], axis=0)
+    ints[...] = (lines + 0.5).astype(jnp.int32)
+    ints[3:4, :FD] = dest[...]
+    ints[4:5, :FD] = part[...]
+    loaded(0, 4)
     first_step(faces, f_col, f_row, f_first, f_send, FD)
 
     @pl.when((sec > 0) & (sec < NS - 1))
@@ -348,12 +386,14 @@
     def _():
         lower_copy().start()
 
+    loaded(9, 13)
     first_step(coarse, c_col, c_row, c_first, c_send, TD)
     start(2, sources[2], landings[2])
     ints_all[me] = ints[...]
     f_all[me] = f_send[me]
     c_all[me] = c_send[me]
 
+    loaded(13, len(loads))
     arrive(0, sources[0], landings[0])
     to_scalar = pltpu.make_async_copy(ints_all, ints_sm, local_sem)
     to_scalar.start()
@@ -368,8 +408,8 @@
 
     def peaks_from(j, _):
         rows = ints_all[j]
-        tables_of(rows[0:1], f_row.shape[1], f_second[...], f_marks[me], f_a, f_cs, j * FD)
-        tables_of(rows[1:2], c_row.shape[1], c_second[...], c_marks[me], c_a, c_cs, j * FD)
+        tables_of(rows[0:1], f_row.shape[1], f_second[...], f_marks, f_a, f_cs, j * FD)
+        tables_of(rows[1:2], c_row.shape[1], c_second[...], c_marks, c_a, c_cs, j * FD)
         return 0
 
     lax.fori_loop(0, T, peaks_from, 0)
@@ -391,7 +431,7 @@
         p, q = both[:rows_s], both[rows_s:]
         return p[:, :n] - q[:, n:], -(p[:, n:] + q[:, :n])
 
-    onehot = jnp.where(iota((n, LANES), 0) == ints[3:4], 1.0, 0.0).astype(jnp.bfloat16)
+    onehot = jnp.where(iota((n, LANES), 0) == ints[2:3], 1.0, 0.0).astype(jnp.bfloat16)
     cs_s = pick(onehot, f_second[...])[TD * PK : 2 * TD * PK]
     a_s = [pick(onehot, s_marks[side])[: TD * PK] for side in range(2)]
     columns = []
@@ -468,7 +508,7 @@
     second_step(f_all, NF, f_second, f_sr, f_si, 2)
     cross_all(
         NF, f_sr, f_si, f_xr, f_xi, f_in, f_sums, lambda p: p,
-        lambda p: ints_sm[p // FD, 2, p % FD] * FD + ints_sm[p // FD, 2, FD + p % FD], f_msg,
+        lambda p: jnp.clip(ints_sm[p // FD, 3, p % FD] * FD + ints_sm[p // FD, 4, p % FD], 0, pairs - 1), f_msg,
     )
     start(3, sources[3], landings[3])
     f_tot[me] = f_msg[...]
@@ -476,7 +516,7 @@
     second_step(c_all, NC, c_second, c_sr, c_si, 2)
     cross_all(
         NC, c_sr, c_si, c_xr, c_xi, c_in, c_sums, lambda p: p // per_tile,
-        lambda p: ints_sm[p // FD, 2, p % FD] * TD + ints_sm[p // FD, 2, FD + p % FD] // per_tile, c_msg,
+        lambda p: jnp.clip(ints_sm[p // FD, 3, p % FD] * TD + ints_sm[p // FD, 4, p % FD] // per_tile, 0, T * TD - 1), c_msg,
     )
     start(4, sources[4], landings[4])
     c_tot[me] = c_msg[...]
@@ -519,18 +559,9 @@
     NF, NC = intersection_faces.shape[-1], coarse.shape[-1]
     pairs = T * FD
 
-    def line(*parts):
-        flat = jnp.concatenate([part.reshape(-1) for part in parts])
-        return jnp.pad(flat, (0, LANES - flat.shape[0]))
-
-    ints = jnp.stack([
-        line(face_peaks[:, 0], face_peaks[:, 1]),
-        line(coarse_peaks[:, 0], coarse_peaks[:, 1]),
-        line(destination, partner),
-        line(section_peaks[:, 0], section_peaks[:, 1]),
-    ] + [jnp.zeros((LANES,), jnp.int32)] * 4)
     operands = [
-        ints, intersection_faces.reshape(FD, NF, NF), coarse,
+        destination.reshape(1, FD), partner.reshape(1, FD), face_peaks, coarse_peaks, section_peaks,
+        intersection_faces.reshape(FD, NF, NF), coarse,
         upper_faces.reshape(TD, NF, NF), lower_faces.reshape(TD, NF, NF),
     ] + [jnp.asarray(t) for t in (
         hann(NF) + hann(NC) + split_tables(NF, T) + split_tables(NC, T) + whole_tables(NF)
@@ -538,7 +569,9 @@
     fr, cr = NF // 2 // T + 8, NC // 2 // T + 8
     f32 = jnp.float32
     V = pltpu.VMEM
-    scratch = [
+    kept = [(x.shape[1:] if x.ndim == 4 else x.shape, x.dtype) for x in operands]
+    scratch = [V(*one) for index, one in enumerate(kept) if index != 8] + [
+        pltpu.SemaphoreType.DMA((len(operands) - 1,)), V((8, LANES), jnp.int32),
         V((T, 8, LANES), jnp.int32), pltpu.SMEM((T, 8, LANES), jnp.int32),
         V((TD, NF, NF), jnp.bfloat16),
         V((T, FD, NF // T, NF), jnp.bfloat16), V((T, FD, NF // T, NF), jnp.bfloat16),
@@ -563,11 +596,11 @@
             jax.ShapeDtypeStruct((FD, PK), f32), jax.ShapeDtypeStruct((FD, PK), f32),
             jax.ShapeDtypeStruct((TD, PK), f32),
         ),
-        in_specs=[pl.BlockSpec(memory_space=pltpu.VMEM)] * len(operands),
+        in_specs=[pl.BlockSpec(memory_space=pltpu.HBM)] * len(operands),
         out_specs=(pl.BlockSpec(memory_space=pltpu.VMEM),) * 3,
         scratch_shapes=scratch,
         compiler_params=pltpu.CompilerParams(
-            collective_id=0, has_side_effects=True, vmem_limit_bytes=44 * 1024 * 1024
+            collective_id=0, has_side_effects=True, vmem_limit_bytes=60 * 1024 * 1024
         ),
     )(*operands)
     return fine.reshape(FD, 1, PK), coarse_scores, section.reshape(TD, 1, PK)

time: 52 us -> 37.6 us (0.72)
  local copies, waits for them, and re-layouts: 16.4 us -> 2.57 us
  Pallas kernels: 33.2 us -> 34.2 us
  other arithmetic: 0.98 us -> 0 us
    unnamed x37 -> x9, local copies, waits for them, and re-layouts: 14.3 us -> 2.57 us
    slice x2 -> x0, local copies, waits for them, and re-layouts: 1.62 us -> none  [the longest x1 0.83 us: split_body(): coarse_peaks[:, 0]]
    pallas_call x1, Pallas kernels: 33.2 us -> 34.2 us  [split_body(): pl.pallas_call(functools.partial(kernel, T, NS), out_shape=(jax.ShapeDtyp...]
    concatenate x2 -> x0, other arithmetic: 0.82 us -> none  [line(): flat = jnp.concatenate([part.reshape(-1) for part in parts])]
where the time goes in v2:
time: 37.6 us; the launch traced here: 37.4 us
  Pallas kernels  34.2 us (91%)
  local copies, waits for them, and re-layouts  2.57 us (7%)
  between operations  0.65 us (2%)
    pallas_call x1, Pallas kernels, split_body(): pl.pallas_call(functools.partial(kernel, T, NS), out_shape=(jax.ShapeDtyp...  34.2 us
    unnamed x9, local copies, waits for them, and re-layouts  2.57 us

profile of v2, /device:TPU:0, one launch (start us, length us, event | category | flops | bytes accessed | tf_op | source)
XLA Modules:
  0.0 37.4 jit_solution(10070633236062002704)
XLA Ops:
  0.6 34.2 %shard_map.229 = (f32[8,8]{1,0:T(8,128)}, f32[8,8]{1,0:T(8,128)}, f32[2,8]{1,0:T(2,128)}) custom-call(s32[1,8]{1,0:T(1,128)} %bitcast.16, s32[1,8]{1,0:T(1,128)} %bitcast.17, s32[8,2,8]{2,1,0:T(2,128)} %h_fp.1, s32[8,2,8]{2,1,0:T(2,128)} %h_cp.1, s32[2,2,8]{2,1,0:T(2,128)} %h_sp.1, bf16[8,128,128]{2,1,0:T(8,128)(2,1)} %bitcast.11, ...), custom_call_target="tpu_custom_call" | custom-call | tf_op jit(solution)/shard_map/pallas_call | solution.py:593
  34.8 0.0 copy-start.1
  34.8 0.7 %copy-done.1 = f32[8,8]{1,0:T(8,128)S(1)} copy-done((f32[8,8]{1,0:T(8,128)S(1)}, f32[8,8]{1,0:T(8,128)}, u32[]{:S(2)}) %copy-start.1) | copy-done | bytes 280
  35.5 0.0 copy-start
  35.5 0.6 %copy.30 = f32[8,1,8]{2,1,0:T(1,128)} copy(f32[8,1,8]{2,1,0:T(1,128)S(1)} %bitcast.14) | data formatting | bytes 512
  36.1 0.1 copy-done
  36.2 0.0 copy-start.2
  36.2 0.6 %copy.31 = f32[8,8]{1,0:T(8,128)} copy(f32[8,8]{1,0:T(8,128)S(1)} %copy-done) | data formatting | bytes 512
  36.8 0.1 copy-done.2
  36.9 0.6 %copy.32 = f32[2,1,8]{2,1,0:T(1,128)} copy(f32[2,1,8]{2,1,0:T(1,128)S(1)} %bitcast.15) | data formatting | bytes 128
Async XLA Ops:
  34.8 0.7 %copy-start.1 = (f32[8,8]{1,0:T(8,128)S(1)}, f32[8,8]{1,0:T(8,128)}, u32[]{:S(2)}) copy-start(f32[8,8]{1,0:T(8,128)} %get-tuple-element.6) | copy-start | bytes 772
  35.5 0.7 %copy-start = (f32[8,8]{1,0:T(8,128)S(1)}, f32[8,8]{1,0:T(8,128)}, u32[]{:S(2)}) copy-start(f32[8,8]{1,0:T(8,128)} %get-tuple-element.16) | copy-start | bytes 772
  36.2 0.7 %copy-start.2 = (f32[2,8]{1,0:T(2,128)S(1)}, f32[2,8]{1,0:T(2,128)}, u32[]{:S(2)}) copy-start(f32[2,8]{1,0:T(2,128)} %get-tuple-element.8) | copy-start | bytes 196

commit v3 on v2

--- a/solution.py
+++ b/solution.py
@@ -412,7 +412,7 @@
         tables_of(rows[1:2], c_row.shape[1], c_second[...], c_marks, c_a, c_cs, j * FD)
         return 0
 
-    lax.fori_loop(0, T, peaks_from, 0)
+    lax.fori_loop(0, T, peaks_from, 0, unroll=4)
 
     @pl.when(sec > 0)
     def _():
@@ -482,7 +482,7 @@
             sums[pl.ds(p, 1), :] = fold(jnp.sum(size * w, axis=0, keepdims=True))
             return 0
 
-        lax.fori_loop(0, pairs, one, 0, unroll=4)
+        lax.fori_loop(0, pairs, one, 0, unroll=8)
         total = jnp.sum(sums[...], axis=1, keepdims=True)
         msg[...] = jnp.broadcast_to(to_row(total, 0), msg.shape)
 
@@ -501,7 +501,7 @@
             part[p] = fold(got[:PK] * table[:, :n] - got[PK:] * table[:, n:])
             return 0
 
-        lax.fori_loop(0, pairs, one, 0, unroll=4)
+        lax.fori_loop(0, pairs, one, 0, unroll=16)
 
     NF, NC = f_row.shape[1], c_row.shape[1]
     arrive(1, sources[1], landings[1])
@@ -534,7 +534,7 @@
         out_msg[j] = jnp.broadcast_to(row, (8, LANES))
         return 0
 
-    lax.fori_loop(0, T, gather, 0)
+    lax.fori_loop(0, T, gather, 0, unroll=8)
     start(5, sources[5], landings[5])
     out_all[me] = out_msg[me]
     for kind in range(5):

time: 37.6 us -> 35.2 us (0.936)
  Pallas kernels: 34.2 us -> 31.8 us
    pallas_call x1, Pallas kernels: 34.2 us -> 31.8 us  [split_body(): pl.pallas_call(functools.partial(kernel, T, NS), out_shape=(jax.ShapeDtyp...]
where the time goes in v3:
time: 35.2 us; the launch traced here: 35 us
  Pallas kernels  31.8 us (90%)
  local copies, waits for them, and re-layouts  2.57 us (7%)
  between operations  0.65 us (2%)
    pallas_call x1, Pallas kernels, split_body(): pl.pallas_call(functools.partial(kernel, T, NS), out_shape=(jax.ShapeDtyp...  31.8 us
    unnamed x9, local copies, waits for them, and re-layouts  2.57 us

profile of v3, /device:TPU:0, one launch (start us, length us, event | category | flops | bytes accessed | tf_op | source)
XLA Modules:
  0.0 35.0 jit_solution(1676928959593923664)
XLA Ops:
  0.6 31.8 %shard_map.229 = (f32[8,8]{1,0:T(8,128)}, f32[8,8]{1,0:T(8,128)}, f32[2,8]{1,0:T(2,128)}) custom-call(s32[1,8]{1,0:T(1,128)} %bitcast.16, s32[1,8]{1,0:T(1,128)} %bitcast.17, s32[8,2,8]{2,1,0:T(2,128)} %h_fp.1, s32[8,2,8]{2,1,0:T(2,128)} %h_cp.1, s32[2,2,8]{2,1,0:T(2,128)} %h_sp.1, bf16[8,128,128]{2,1,0:T(8,128)(2,1)} %bitcast.11, ...), custom_call_target="tpu_custom_call" | custom-call | tf_op jit(solution)/shard_map/pallas_call | solution.py:593
  32.4 0.0 copy-start.1
  32.5 0.7 %copy-done.1 = f32[8,8]{1,0:T(8,128)S(1)} copy-done((f32[8,8]{1,0:T(8,128)S(1)}, f32[8,8]{1,0:T(8,128)}, u32[]{:S(2)}) %copy-start.1) | copy-done | bytes 280
  33.1 0.0 copy-start
  33.1 0.6 %copy.30 = f32[8,1,8]{2,1,0:T(1,128)} copy(f32[8,1,8]{2,1,0:T(1,128)S(1)} %bitcast.14) | data formatting | bytes 512
  33.7 0.1 copy-done
  33.8 0.0 copy-start.2
  33.8 0.6 %copy.31 = f32[8,8]{1,0:T(8,128)} copy(f32[8,8]{1,0:T(8,128)S(1)} %copy-done) | data formatting | bytes 512
  34.4 0.1 copy-done.2
  34.5 0.6 %copy.32 = f32[2,1,8]{2,1,0:T(1,128)} copy(f32[2,1,8]{2,1,0:T(1,128)S(1)} %bitcast.15) | data formatting | bytes 128
Async XLA Ops:
  32.4 0.7 %copy-start.1 = (f32[8,8]{1,0:T(8,128)S(1)}, f32[8,8]{1,0:T(8,128)}, u32[]{:S(2)}) copy-start(f32[8,8]{1,0:T(8,128)} %get-tuple-element.6) | copy-start | bytes 772
  33.1 0.7 %copy-start = (f32[8,8]{1,0:T(8,128)S(1)}, f32[8,8]{1,0:T(8,128)}, u32[]{:S(2)}) copy-start(f32[8,8]{1,0:T(8,128)} %get-tuple-element.16) | copy-start | bytes 772
  33.8 0.7 %copy-start.2 = (f32[2,8]{1,0:T(2,128)S(1)}, f32[2,8]{1,0:T(2,128)}, u32[]{:S(2)}) copy-start(f32[2,8]{1,0:T(2,128)} %get-tuple-element.8) | copy-start | bytes 196

commit v4 on v3

--- a/solution.py
+++ b/solution.py
@@ -414,6 +414,95 @@
 
     lax.fori_loop(0, T, peaks_from, 0, unroll=4)
 
+    to_scalar.wait()
+
+    def second_step(block, n, second, sr, si, groups):
+        rows = n // 2 // T
+        per = T // groups
+        images = block.shape[1]
+        for group in range(groups):
+            x = block[group * per : (group + 1) * per].reshape(per * images * 2 * rows, n)
+            both = mm(x, second[...]).reshape(per * images, 2 * rows, 2 * n)
+            p, q = both[:, :rows], both[:, rows:]
+            special = (iota((1, rows, 1), 1) == 0) & (me == 0)
+            at = slice(group * per * images, (group + 1) * per * images)
+            sr[at, :rows, :] = p[:, :, :n] - jnp.where(special, 0.0, q[:, :, n:])
+            si[at, :rows, :] = -(p[:, :, n:] + jnp.where(special, 0.0, q[:, :, :n]))
+            sr[at, rows:, :] = q[:, :8, :n]
+            si[at, rows:, :] = -q[:, :8, n:]
+
+    def weights(rows, n):
+        at = iota((rows + 8, n), 0)
+        main = jnp.where((at == 0) & (me == 0), 1.0, 2.0)
+        extra = jnp.where((at == rows) & (me == 0), 1.0, 0.0)
+        return jnp.where(at < rows, main, extra)
+
+    def cross_all(n, sr, si, xr, xi, inv, sums, own_of, other_of, msg):
+        w = weights(n // 2 // T, n)
+
+        def one(p, _):
+            own, other = own_of(p), other_of(p)
+            vr, vi, inverse, size = cross(sr[own], si[own], sr[other], si[other])
+            xr[p], xi[p], inv[p] = vr, vi, inverse
+            sums[pl.ds(p, 1), :] = fold(jnp.sum(size * w, axis=0, keepdims=True))
+            return 0
+
+        lax.fori_loop(0, pairs, one, 0, unroll=8)
+        total = jnp.sum(sums[...], axis=1, keepdims=True)
+        msg[...] = jnp.broadcast_to(to_row(total, 0), msg.shape)
+
+    def score_all(n, tot, it, xr, xi, inv, a, cs, part):
+        row = jnp.sum(tot[...], axis=0)[0:1]
+        limit = 1.0 / (row * (0.05 / (n * n)) + 1e-6)
+        shape = (pairs, LANES)
+        column = jnp.sum(jnp.where(iota(shape, 1) == iota(shape, 0), limit, 0.0), axis=1, keepdims=True)
+        it[...] = jnp.broadcast_to(column, it.shape)
+
+        def one(p, _):
+            scale = jnp.minimum(inv[p], it[pl.ds(p, 1), :])
+            unit = jnp.concatenate([xr[p] * scale, xi[p] * scale], axis=0).astype(jnp.bfloat16)
+            got = mm(a[p].astype(jnp.bfloat16), unit)
+            table = cs[p]
+            part[p] = fold(got[:PK] * table[:, :n] - got[PK:] * table[:, n:])
+            return 0
+
+        lax.fori_loop(0, pairs, one, 0, unroll=16)
+
+    NF, NC = f_row.shape[1], c_row.shape[1]
+    arrive(1, sources[1], landings[1])
+    second_step(f_all, NF, f_second, f_sr, f_si, 2)
+    cross_all(
+        NF, f_sr, f_si, f_xr, f_xi, f_in, f_sums, lambda p: p,
+        lambda p: jnp.clip(ints_sm[p // FD, 3, p % FD] * FD + ints_sm[p // FD, 4, p % FD], 0, pairs - 1), f_msg,
+    )
+    start(3, sources[3], landings[3])
+    f_tot[me] = f_msg[...]
+    arrive(2, sources[2], landings[2])
+    second_step(c_all, NC, c_second, c_sr, c_si, 2)
+    cross_all(
+        NC, c_sr, c_si, c_xr, c_xi, c_in, c_sums, lambda p: p // per_tile,
+        lambda p: jnp.clip(ints_sm[p // FD, 3, p % FD] * TD + ints_sm[p // FD, 4, p % FD] // per_tile, 0, T * TD - 1), c_msg,
+    )
+    start(4, sources[4], landings[4])
+    c_tot[me] = c_msg[...]
+    arrive(3, sources[3], landings[3])
+    score_all(NF, f_tot, f_it, f_xr, f_xi, f_in, f_a, f_cs, f_part)
+    arrive(4, sources[4], landings[4])
+    score_all(NC, c_tot, c_it, c_xr, c_xi, c_in, c_a, c_cs, c_part)
+
+    def gather(j, _):
+        def column(part):
+            block = part[pl.ds(j * FD, FD)].reshape(FD * PK, LANES)
+            return jnp.sum(block, axis=1, keepdims=True)
+
+        row = to_row(column(c_part), 0) + to_row(column(f_part), FD * PK)
+        out_msg[j] = jnp.broadcast_to(row, (8, LANES))
+        return 0
+
+    lax.fori_loop(0, T, gather, 0, unroll=8)
+    start(5, sources[5], landings[5])
+    out_all[me] = out_msg[me]
+
     @pl.when(sec > 0)
     def _():
         lower_copy().wait_recv()
@@ -449,94 +538,6 @@
     row = to_row(jnp.concatenate(columns, axis=0), 0)
     section_out[...] = to_grid(jnp.broadcast_to(row, (8, LANES)), 0, PK)[:TD] * (1.0 / n)
 
-    to_scalar.wait()
-
-    def second_step(block, n, second, sr, si, groups):
-        rows = n // 2 // T
-        per = T // groups
-        images = block.shape[1]
-        for group in range(groups):
-            x = block[group * per : (group + 1) * per].reshape(per * images * 2 * rows, n)
-            both = mm(x, second[...]).reshape(per * images, 2 * rows, 2 * n)
-            p, q = both[:, :rows], both[:, rows:]
-            special = (iota((1, rows, 1), 1) == 0) & (me == 0)
-            at = slice(group * per * images, (group + 1) * per * images)
-            sr[at, :rows, :] = p[:, :, :n] - jnp.where(special, 0.0, q[:, :, n:])
-            si[at, :rows, :] = -(p[:, :, n:] + jnp.where(special, 0.0, q[:, :, :n]))
-            sr[at, rows:, :] = q[:, :8, :n]
-            si[at, rows:, :] = -q[:, :8, n:]
-
-    def weights(rows, n):
-        at = iota((rows + 8, n), 0)
-        main = jnp.where((at == 0) & (me == 0), 1.0, 2.0)
-        extra = jnp.where((at == rows) & (me == 0), 1.0, 0.0)
-        return jnp.where(at < rows, main, extra)
-
-    def cross_all(n, sr, si, xr, xi, inv, sums, own_of, other_of, msg):
-        w = weights(n // 2 // T, n)
-
-        def one(p, _):
-            own, other = own_of(p), other_of(p)
-            vr, vi, inverse, size = cross(sr[own], si[own], sr[other], si[other])
-            xr[p], xi[p], inv[p] = vr, vi, inverse
-            sums[pl.ds(p, 1), :] = fold(jnp.sum(size * w, axis=0, keepdims=True))
-            return 0
-
-        lax.fori_loop(0, pairs, one, 0, unroll=8)
-        total = jnp.sum(sums[...], axis=1, keepdims=True)
-        msg[...] = jnp.broadcast_to(to_row(total, 0), msg.shape)
-
-    def score_all(n, tot, it, xr, xi, inv, a, cs, part):
-        row = jnp.sum(tot[...], axis=0)[0:1]
-        limit = 1.0 / (row * (0.05 / (n * n)) + 1e-6)
-        shape = (pairs, LANES)
-        column = jnp.sum(jnp.where(iota(shape, 1) == iota(shape, 0), limit, 0.0), axis=1, keepdims=True)
-        it[...] = jnp.broadcast_to(column, it.shape)
-
-        def one(p, _):
-            scale = jnp.minimum(inv[p], it[pl.ds(p, 1), :])
-            unit = jnp.concatenate([xr[p] * scale, xi[p] * scale], axis=0).astype(jnp.bfloat16)
-            got = mm(a[p].astype(jnp.bfloat16), unit)
-            table = cs[p]
-            part[p] = fold(got[:PK] * table[:, :n] - got[PK:] * table[:, n:])
-            return 0
-
-        lax.fori_loop(0, pairs, one, 0, unroll=16)
-
-    NF, NC = f_row.shape[1], c_row.shape[1]
-    arrive(1, sources[1], landings[1])
-    second_step(f_all, NF, f_second, f_sr, f_si, 2)
-    cross_all(
-        NF, f_sr, f_si, f_xr, f_xi, f_in, f_sums, lambda p: p,
-        lambda p: jnp.clip(ints_sm[p // FD, 3, p % FD] * FD + ints_sm[p // FD, 4, p % FD], 0, pairs - 1), f_msg,
-    )
-    start(3, sources[3], landings[3])
-    f_tot[me] = f_msg[...]
-    arrive(2, sources[2], landings[2])
-    second_step(c_all, NC, c_second, c_sr, c_si, 2)
-    cross_all(
-        NC, c_sr, c_si, c_xr, c_xi, c_in, c_sums, lambda p: p // per_tile,
-        lambda p: jnp.clip(ints_sm[p // FD, 3, p % FD] * TD + ints_sm[p // FD, 4, p % FD] // per_tile, 0, T * TD - 1), c_msg,
-    )
-    start(4, sources[4], landings[4])
-    c_tot[me] = c_msg[...]
-    arrive(3, sources[3], landings[3])
-    score_all(NF, f_tot, f_it, f_xr, f_xi, f_in, f_a, f_cs, f_part)
-    arrive(4, sources[4], landings[4])
-    score_all(NC, c_tot, c_it, c_xr, c_xi, c_in, c_a, c_cs, c_part)
-
-    def gather(j, _):
-        def column(part):
-            block = part[pl.ds(j * FD, FD)].reshape(FD * PK, LANES)
-            return jnp.sum(block, axis=1, keepdims=True)
-
-        row = to_row(column(c_part), 0) + to_row(column(f_part), FD * PK)
-        out_msg[j] = jnp.broadcast_to(row, (8, LANES))
-        return 0
-
-    lax.fori_loop(0, T, gather, 0, unroll=8)
-    start(5, sources[5], landings[5])
-    out_all[me] = out_msg[me]
     for kind in range(5):
         sent(kind, sources[kind], landings[kind])
 

time: 35.2 us -> 35.2 us (level)
  no operation moved by 1% of the time
where the time goes in v4:
time: 35.2 us; the launch traced here: 35 us
  Pallas kernels  31.8 us (90%)
  local copies, waits for them, and re-layouts  2.57 us (7%)
  between operations  0.65 us (2%)
    pallas_call x1, Pallas kernels, split_body(): pl.pallas_call(functools.partial(kernel, T, NS), out_shape=(jax.ShapeDtyp...  31.8 us
    unnamed x9, local copies, waits for them, and re-layouts  2.57 us

profile of v4, /device:TPU:0, one launch (start us, length us, event | category | flops | bytes accessed | tf_op | source)
XLA Modules:
  0.0 35.0 jit_solution(13043501217094268863)
XLA Ops:
  0.6 31.8 %shard_map.229 = (f32[8,8]{1,0:T(8,128)}, f32[8,8]{1,0:T(8,128)}, f32[2,8]{1,0:T(2,128)}) custom-call(s32[1,8]{1,0:T(1,128)} %bitcast.16, s32[1,8]{1,0:T(1,128)} %bitcast.17, s32[8,2,8]{2,1,0:T(2,128)} %h_fp.1, s32[8,2,8]{2,1,0:T(2,128)} %h_cp.1, s32[2,2,8]{2,1,0:T(2,128)} %h_sp.1, bf16[8,128,128]{2,1,0:T(8,128)(2,1)} %bitcast.11, ...), custom_call_target="tpu_custom_call" | custom-call | tf_op jit(solution)/shard_map/pallas_call | solution.py:594
  32.4 0.0 copy-start.1
  32.4 0.7 %copy-done.1 = f32[8,8]{1,0:T(8,128)S(1)} copy-done((f32[8,8]{1,0:T(8,128)S(1)}, f32[8,8]{1,0:T(8,128)}, u32[]{:S(2)}) %copy-start.1) | copy-done | bytes 280
  33.1 0.0 copy-start
  33.1 0.6 %copy.30 = f32[8,1,8]{2,1,0:T(1,128)} copy(f32[8,1,8]{2,1,0:T(1,128)S(1)} %bitcast.14) | data formatting | bytes 512
  33.7 0.1 copy-done
  33.8 0.0 copy-start.2
  33.8 0.6 %copy.31 = f32[8,8]{1,0:T(8,128)} copy(f32[8,8]{1,0:T(8,128)S(1)} %copy-done) | data formatting | bytes 512
  34.4 0.1 copy-done.2
  34.4 0.6 %copy.32 = f32[2,1,8]{2,1,0:T(1,128)} copy(f32[2,1,8]{2,1,0:T(1,128)S(1)} %bitcast.15) | data formatting | bytes 128
Async XLA Ops:
  32.4 0.7 %copy-start.1 = (f32[8,8]{1,0:T(8,128)S(1)}, f32[8,8]{1,0:T(8,128)}, u32[]{:S(2)}) copy-start(f32[8,8]{1,0:T(8,128)} %get-tuple-element.6) | copy-start | bytes 772
  33.1 0.7 %copy-start = (f32[8,8]{1,0:T(8,128)S(1)}, f32[8,8]{1,0:T(8,128)}, u32[]{:S(2)}) copy-start(f32[8,8]{1,0:T(8,128)} %get-tuple-element.16) | copy-start | bytes 772
  33.8 0.7 %copy-start.2 = (f32[2,8]{1,0:T(2,128)S(1)}, f32[2,8]{1,0:T(2,128)}, u32[]{:S(2)}) copy-start(f32[2,8]{1,0:T(2,128)} %get-tuple-element.8) | copy-start | bytes 196
